TPU v7x, 512 devices: a whole 4x8x8 slice. The times are simulated.
512 devices in a mesh: dp: 128 (over z_lo, x, y), slab: 4 (over z_hi, core).
Axes of the slice: x: 4, y: 8, z: 8 (z_hi: 2, z_lo: 4; z = z_hi * 4 + z_lo), core: 2. Of those that a mesh axis runs over, the one named last changes fastest.
Arguments:
- features: bfloat16 [128, 48, 40, 2048], P('dp', 'slab'), may hold values from -6 to 6
- labels: int32 [128, 48, 40], P('dp', 'slab'), may hold values from 0 to 2
- cotangent: bfloat16 [128, 48, 40, 256], P('dp', 'slab'), may hold values from -6 to 6
- first_kernel: float32 [3, 3, 2048], replicated, may hold values from -2 to 2
- holed_kernel: float32 [3, 3, 2048], replicated, may hold values from -2 to 2
- point_weight: bfloat16 [2048, 256], replicated, may hold values from -0.125 to 0.125
Outputs:
- branch_out: bfloat16 [128, 48, 40, 256], P('dp', 'slab')
- point_grad: bfloat16 [2048, 256], replicated
- first_grad: float32 [3, 3, 2048], replicated
- atrous_grad: float32 [3, 3, 2048], replicated
All inputs are finite; a program needn't handle non-finite values.
Results may differ from a plain program's by a relative error of at most 0.015.
Values may be sent and summed in bfloat16 or wider, within the bound.
No kernel may reach another device: no remote copies, remote signals or barrier semaphores. Data moves between devices by JAX's collectives and lax.ppermute only.
A program may use at most 128 MiB of HBM per device.

v0:
```python
import math
import jax
import jax.numpy as jnp
from jax import lax
from jax.sharding import PartitionSpec as P

DILATION_STEP = 36


def from_behind(value, axis, steps):
    count = lax.axis_size(axis)
    initial, last = (max(0, -steps), min(count, count - steps))
    return lax.ppermute(value, axis, [(source, source + steps) for source in range(initial, last)])


def extended(block, sides, width):
    for axis, dim in sides:
        count = lax.axis_size(axis)
        forward = [(i, i + 1) for i in range(count - 1)]
        backward = [(target, source) for source, target in forward]
        low = lax.ppermute(
            lax.slice_in_dim(block, block.shape[dim] - width, None, axis=dim), axis, forward
        )
        high = lax.ppermute(lax.slice_in_dim(block, 0, width, axis=dim), axis, backward)
        block = jnp.concatenate([low, block, high], axis=dim)
    return block


def class_weighting(labels):
    return jnp.where(labels == 0, 0.6, jnp.where(labels == 1, 2.4, 1.5)).astype(jnp.float32)


def kernel_tap_window(padded, kernel, row_count, column_count, stride):
    summed = jnp.zeros((row_count, column_count, padded.shape[2]), jnp.float32)
    for row_tap in range(3):
        for col_tap in range(3):
            window = padded[
                row_tap * stride : row_tap * stride + row_count,
                col_tap * stride : col_tap * stride + column_count,
            ]
            summed = summed + kernel[row_tap, col_tap] * window
    return summed


def kernel_tap_product(padded, gradient, row_count, column_count, stride):
    pieces = []
    for row_tap in range(3):
        for col_tap in range(3):
            window = padded[
                row_tap * stride : row_tap * stride + row_count,
                col_tap * stride : col_tap * stride + column_count,
            ]
            pieces.append(jnp.sum(window * gradient, axis=(0, 1)))
    return jnp.stack(pieces).reshape(3, 3, -1)


def widen_cols(slab_block, stride):
    return jnp.pad(slab_block[0].astype(jnp.float32), ((0, 0), (stride, stride), (0, 0)))


def holed_rows(blocks, kernel, column_count, stride):
    summed = jnp.zeros(blocks[1].shape[1:], jnp.float32)
    for row_tap in range(3):
        widened = widen_cols(blocks[row_tap], stride)
        for col_tap in range(3):
            summed = (
                summed
                + kernel[row_tap, col_tap]
                * widened[:, col_tap * stride : col_tap * stride + column_count]
            )
    return summed


def holed_multiply(blocks, gradient, column_count, stride):
    pieces = []
    for row_tap in range(3):
        widened = widen_cols(blocks[row_tap], stride)
        for col_tap in range(3):
            window = widened[:, col_tap * stride : col_tap * stride + column_count]
            pieces.append(jnp.sum(window * gradient, axis=(0, 1)))
    return jnp.stack(pieces).reshape(3, 3, -1)


def far_rows(slab_block):
    halo_extent = DILATION_STEP // slab_block.shape[1]
    from_above = from_behind(slab_block, "slab", halo_extent)
    from_below = from_behind(slab_block, "slab", -halo_extent)
    return (from_above, from_below)


def per_device(features, labels, cotangent, first_kernel, holed_kernel, point_weight):
    row_count = features.shape[1]
    column_count = features.shape[2]
    channels = features.shape[3]
    out_width = point_weight.shape[1]
    reversed_kernel = holed_kernel[::-1, ::-1]
    scale_factor = 1.0 / math.sqrt(
        lax.axis_size("dp") * lax.axis_size("slab") * row_count * column_count
    )
    weighting = class_weighting(labels[0])[:, :, None]
    weighted = (cotangent[0].astype(jnp.float32) * weighting).astype(jnp.bfloat16)
    weighted_flat = weighted.reshape(row_count * column_count, out_width)
    bordered = extended(features, (("slab", 1),), 1)
    padded_in = jnp.pad(bordered[0].astype(jnp.float32), ((0, 0), (1, 1), (0, 0)))
    first = kernel_tap_window(padded_in, first_kernel, row_count, column_count, 1).astype(
        jnp.bfloat16
    )[None]
    first_above, first_below = far_rows(first)
    leading_blocks = (first_above, first, first_below)
    holed_output = holed_rows(leading_blocks, holed_kernel, column_count, DILATION_STEP).astype(
        jnp.bfloat16
    )[None]
    atrous_flat = holed_output.reshape(row_count * column_count, channels)
    branch_out = jnp.dot(atrous_flat, point_weight, preferred_element_type=jnp.float32).astype(
        jnp.bfloat16
    )
    branch_out = branch_out.reshape(1, row_count, column_count, out_width)
    holed_gradient = lax.dot_general(
        weighted_flat, point_weight, (((1,), (1,)), ((), ())), preferred_element_type=jnp.float32
    ).astype(jnp.bfloat16)
    point_part = lax.dot_general(
        atrous_flat, weighted_flat, (((0,), (0,)), ((), ())), preferred_element_type=jnp.float32
    )
    holed_gradient = holed_gradient.reshape(1, row_count, column_count, channels)
    gradient_widened = holed_gradient[0].astype(jnp.float32)
    gradient_upper_halo, gradient_lower_halo = far_rows(holed_gradient)
    holed_portion = holed_multiply(leading_blocks, gradient_widened, column_count, DILATION_STEP)
    leading_gradient = holed_rows(
        (gradient_upper_halo, holed_gradient, gradient_lower_halo),
        reversed_kernel,
        column_count,
        DILATION_STEP,
    ).astype(jnp.bfloat16)
    first_part = kernel_tap_product(
        padded_in, leading_gradient.astype(jnp.float32), row_count, column_count, 1
    )
    point_sum, first_sum, holed_total_sum = lax.psum(
        (point_part, first_part, holed_portion), ("dp", "slab")
    )
    point_grad = (point_sum * scale_factor).astype(jnp.bfloat16)
    return (branch_out, point_grad, first_sum * scale_factor, holed_total_sum * scale_factor)


def solution(mesh):
    in_specs = (
        P("dp", "slab", None, None),
        P("dp", "slab", None),
        P("dp", "slab", None, None),
        P(),
        P(),
        P(),
    )
    out_specs = (P("dp", "slab", None, None), P(), P(), P())
    return jax.shard_map(
        per_device, mesh=mesh, in_specs=in_specs, out_specs=out_specs, check_vma=False
    )
```

profile of v0, /device:TPU:17, one launch (start us, length us, event | category | flops | bytes accessed | tf_op | source)
XLA Modules:
  0.0 424.9 jit_solution(1523050457168167211)
XLA Ops:
  7.2 0.8 fusion.39
  8.1 0.1 select_n.29
  8.2 1.2 fusion.33
  9.4 0.7 convolution_convert_fusion
  10.1 1.9 collective-permute-start.5
  12.1 1.9 collective-permute-start.4
  14.0 11.2 %collective-permute-start = (bf16[1,1,40,2048]{3,2,1,0:T(8,128)(2,1)S(1)}, bf16[1,1,40,2048]{3,2,1,0:T(8,128)(2,1)S(1)}, u32[]{:S(2)}, u32[]{:S(2)}) collective-permute-start(bf16[1,1,40,2048]{3,2,1,0:T(8,128)(2,1)S(1)} %get-tuple-element.38), channel_id=1, source_target_pairs={{0,1},{1,2},{2,3},{4,5},{5,6},{6,7},{8,9},{9,10},{10,11},{12,13},{... | collective-permute-start | bytes 491528 | tf_op jit(solution)/shard_map/ppermute | solution.py:21
  25.2 3.0 collective-permute-start.1
  28.2 0.1 fusion.43
  28.4 2.4 convert.10
  30.7 7.2 %collective-permute-done.1 = bf16[1,1,40,2048]{3,2,1,0:T(8,128)(2,1)S(1)} collective-permute-done((bf16[1,1,40,2048]{3,2,1,0:T(8,128)(2,1)S(1)}, bf16[1,1,40,2048]{3,2,1,0:T(8,128)(2,1)S(1)}, u32[]{:S(2)}, u32[]{:S(2)}) %collective-permute-start.1) | collective-permute-done | bytes 163872 | tf_op jit(solution)/shard_map/ppermute | solution.py:24
  38.0 2.6 fusion.38
  40.6 13.2 %fusion.40 = (f32[12,40,2048]{2,1,0:T(8,128)}, bf16[12,40,2048]{2,1,0:T(8,128)(2,1)}) fusion(f32[2048]{0:T(1024)S(1)} %bitcast.133, f32[1,14,40,2048]{3,2,1,0:T(8,128)S(1)} %get-tuple-element.37, f32[2048]{0:T(1024)S(1)} %bitcast.134, f32[2048]{0:T(1024)S(1)} %bitcast.127, f32[2048]{0:T(1024)S(1)} %bitcast.128, f32[2048]{0:T(1024)S(1)} %bitcast.129, ...), kind=kLoop, calls=%fused_computation.97 | loop fusion | flops 18677760 | bytes 22355968 | tf_op jit(solution)/shard_map/convert_element_type | solution.py:58
  53.9 2.0 collective-permute-start.3
  55.8 2.0 collective-permute-start.2
  57.8 3.9 bitcast_convert_fusion
  61.7 3.9 bitcast_convert_fusion.1
  65.6 16.6 %fusion.23 = (f32[2048]{0:T(1024)S(1)}, f32[2048]{0:T(1024)S(1)}, f32[2048]{0:T(1024)S(1)}, f32[2048]{0:T(1024)S(1)}, f32[2048]{0:T(1024)S(1)}, /*index=5*/f32[2...) fusion(f32[14,40,2048]{2,1,0:T(8,128)} %get-tuple-element.36, ...), kind=kLoop, calls=%fused_computation.60 | loop fusion | flops 37337088 | bytes 30294016 | tf_op jit(solution)/shard_map/reduce_sum | solution.py:53
  82.3 0.1 stack.69
  82.4 0.7 reshape.75
  83.1 2.0 bitcast_convert_fusion.3
  85.1 2.2 bitcast_convert_fusion.2
  87.3 0.5 copy-done.1
  87.8 3.3 add_convert_fusion
  91.2 4.6 %fusion.14 = (f32[2048]{0:T(1024)S(1)}, f32[2048]{0:T(1024)S(1)}, f32[2048]{0:T(1024)S(1)}, f32[2048]{0:T(1024)S(1)}, f32[2048]{0:T(1024)S(1)}, /*index=5*/f32[2...) fusion(bf16[12,40,2048]{2,1,0:T(8,128)(2,1)S(1)} %bitcast.104, ...), kind=kLoop, calls=%fused_computation.51 | loop fusion | flops 21608448 | bytes 19734528 | tf_op jit(solution)/shard_map/reduce_sum | solution.py:80
  95.7 0.1 stack.79
  95.8 0.7 reshape.76
  96.5 3.8 convolution_bitcast_fusion
  100.4 1.4 convolution_convert_fusion.1
  101.8 311.9 %all-reduce.10.cloned.1.call-done = (f32[2048,256]{1,0:T(8,128)}, f32[3,3,2048]{2,1,0:T(4,128)}, f32[3,3,2048]{2,1,0:T(4,128)}) async-done(((f32[2048,256]{1,0:T(8,128)}, f32[3,3,2048]{2,1,0:T(4,128)}, f32[3,3,2048]{2,1,0:T(4,128)}), (f32[2048,256]{1,0:T(8,128)}, f32[3,3,2048]{2,1,0:T(4,128)}, f32[3,3,2048]{2,1,0:T(4,128)})) %all-reduce.10.cloned.1.call-update) | async-done | bytes 2244624 | tf_op jit(solution)/shard_map/psum | solution.py:137
  413.6 2.8 multiply_convert_fusion
  416.4 1.7 broadcast_multiply_fusion
  (25 shorter events, 0.2 us)
Async XLA Ops:
  7.2 2.2 copy-start
  7.2 21.0 %copy-start.6 = (f32[3,3,2048]{2,1,0:T(4,128)S(1)}, f32[3,3,2048]{2,1,0:T(4,128)}, u32[]{:S(2)}) copy-start(f32[3,3,2048]{2,1,0:T(4,128)} %param.9) | copy-start | bytes 221188
  7.2 21.1 %copy-start.7 = (f32[3,3,2048]{2,1,0:T(4,128)S(1)}, f32[3,3,2048]{2,1,0:T(4,128)}, u32[]{:S(2)}) copy-start(f32[3,3,2048]{2,1,0:T(4,128)} %param.10) | copy-start | bytes 221188
  7.2 406.4 %all-reduce.10.cloned.1.call-start = ((), (), s32[]{:S(2)}) async-start(), calls=%async_computation | async-start | bytes 4587520 | tf_op jit(solution)/shard_map/psum | solution.py:137
  8.1 5.8 %copy-start.3 = (bf16[1,12,40,2048]{3,2,1,0:T(8,128)(2,1)S(1)}, bf16[1,12,40,2048]{3,2,1,0:T(8,128)(2,1)}, u32[]{:S(2)}) copy-start(bf16[1,12,40,2048]{3,2,1,0:T(8,128)(2,1)} %param.6) | copy-start | bytes 5898244
  10.1 47.7 %collective-permute-start.5 = (bf16[1,12,40,2048]{3,2,1,0:T(8,128)(2,1)S(1)}, bf16[1,12,40,2048]{3,2,1,0:T(8,128)(2,1)}, u32[]{:S(2)}, u32[]{:S(2)}) collective-permute-start(bf16[1,12,40,2048]{3,2,1,0:T(8,128)(2,1)S(1)} %bitcast.100), channel_id=1, source_target_pairs={{3,0},{7,4},{11,8},{15,12},{19,16},{23,20},{27,24},{31,28},{35,32}... | collective-permute-start | bytes 5898248 | tf_op jit(solution)/shard_map/ppermute | solution.py:13
  12.1 49.7 %collective-permute-start.4 = (bf16[1,12,40,2048]{3,2,1,0:T(8,128)(2,1)S(1)}, bf16[1,12,40,2048]{3,2,1,0:T(8,128)(2,1)}, u32[]{:S(2)}, u32[]{:S(2)}) collective-permute-start(bf16[1,12,40,2048]{3,2,1,0:T(8,128)(2,1)S(1)} %bitcast.101), channel_id=1, source_target_pairs={{0,3},{4,7},{8,11},{12,15},{16,19},{20,23},{24,27},{28,31},{32,35}... | collective-permute-start | bytes 5898248 | tf_op jit(solution)/shard_map/ppermute | solution.py:13
  14.0 16.7 %collective-permute-start = (bf16[1,1,40,2048]{3,2,1,0:T(8,128)(2,1)S(1)}, bf16[1,1,40,2048]{3,2,1,0:T(8,128)(2,1)S(1)}, u32[]{:S(2)}, u32[]{:S(2)}) collective-permute-start(bf16[1,1,40,2048]{3,2,1,0:T(8,128)(2,1)S(1)} %get-tuple-element.38), channel_id=1, source_target_pairs={{0,1},{1,2},{2,3},{4,5},{5,6},{6,7},{8,9},{9,10},{10,11},{12,13},{... | collective-permute-start | bytes 491528 | tf_op jit(solution)/shard_map/ppermute | solution.py:21
  25.2 12.8 %collective-permute-start.1 = (bf16[1,1,40,2048]{3,2,1,0:T(8,128)(2,1)S(1)}, bf16[1,1,40,2048]{3,2,1,0:T(8,128)(2,1)S(1)}, u32[]{:S(2)}, u32[]{:S(2)}) collective-permute-start(bf16[1,1,40,2048]{3,2,1,0:T(8,128)(2,1)S(1)} %get-tuple-element.39), channel_id=1, source_target_pairs={{1,0},{2,1},{3,2},{5,4},{6,5},{7,6},{9,8},{10,9},{11,10},{13,12},{... | collective-permute-start | bytes 491528 | tf_op jit(solution)/shard_map/ppermute | solution.py:24
  53.9 31.3 %collective-permute-start.3 = (bf16[1,12,40,2048]{3,2,1,0:T(8,128)(2,1)}, bf16[1,12,40,2048]{3,2,1,0:T(8,128)(2,1)}, u32[]{:S(2)}, u32[]{:S(2)}) collective-permute-start(bf16[1,12,40,2048]{3,2,1,0:T(8,128)(2,1)} %bitcast.105), channel_id=1, source_target_pairs={{3,0},{7,4},{11,8},{15,12},{19,16},{23,20},{27,24},{31,28},{35,32}... | collective-permute-start | bytes 5898248 | tf_op jit(solution)/shard_map/ppermute | solution.py:13
  55.8 27.3 %collective-permute-start.2 = (bf16[1,12,40,2048]{3,2,1,0:T(8,128)(2,1)}, bf16[1,12,40,2048]{3,2,1,0:T(8,128)(2,1)}, u32[]{:S(2)}, u32[]{:S(2)}) collective-permute-start(bf16[1,12,40,2048]{3,2,1,0:T(8,128)(2,1)} %bitcast.106), channel_id=1, source_target_pairs={{0,3},{4,7},{8,11},{12,15},{16,19},{20,23},{24,27},{28,31},{32,35}... | collective-permute-start | bytes 5898248 | tf_op jit(solution)/shard_map/ppermute | solution.py:13
  85.1 2.7 copy-start.1
  87.8 3.3 copy-start.2
  91.2 5.4 %copy-start.5 = (bf16[1,12,40,256]{3,2,1,0:T(8,128)(2,1)S(1)}, bf16[1,12,40,256]{3,2,1,0:T(8,128)(2,1)}, u32[]{:S(2)}) copy-start(bf16[1,12,40,256]{3,2,1,0:T(8,128)(2,1)} %param.8) | copy-start | bytes 737284
  96.5 3.9 copy-start.4
Sparse Core Ops, SparseCore 0:
  100.5 313.0 all-reduce.9
where the time goes:
time: 425 us
  waiting for transfers between devices  319 us (75%)
  other arithmetic  61.2 us (14%)
  starting transfers between devices  22.1 us (5%)
  between operations  14.2 us (3%)
  matrix products  5.92 us (1%)
    psum x1, waiting for transfers between devices, per_device(): lax.psum((point_part, first_part, holed_portion), ('dp', 'slab'))  312 us
    convert_element_type x6, other arithmetic, widen_cols(): slab_block[0].astype(jnp.float32)  27.6 us
    reduce_sum x1, other arithmetic, kernel_tap_product(): pieces.append(jnp.sum(window * gradient, axis=(0, 1)))  16.6 us
    ppermute x1, starting transfers between devices, extended(): lax.ppermute(lax.slice_in_dim(block, block.shape[dim] - width, None, axis...  11.2 us
  transfers between devices with their start and end apart: 7, of which 2 were waited for; matrix products, arithmetic and copies ran while one was open for 11% of the time, Pallas kernels for 0%

commit v1 on v0

--- a/solution.py
+++ b/solution.py
@@ -135,7 +135,7 @@
         padded_in, leading_gradient.astype(jnp.float32), row_count, column_count, 1
     )
     point_sum, first_sum, holed_total_sum = lax.psum(
-        (point_part, first_part, holed_portion), ("dp", "slab")
+        lax.psum((point_part, first_part, holed_portion), "slab"), "dp"
     )
     point_grad = (point_sum * scale_factor).astype(jnp.bfloat16)
     return (branch_out, point_grad, first_sum * scale_factor, holed_total_sum * scale_factor)

time: 425 us -> 1620 us (3.81)
  the two profiles are of different devices: /device:TPU:17 before, /device:TPU:8 now
where the time goes in v1:
time: 1620 us
  waiting for transfers between devices  1510 us (93%)
  other arithmetic  61.2 us (4%)
  starting transfers between devices  28.9 us (2%)
    psum x1, waiting for transfers between devices, per_device(): lax.psum(lax.psum((point_part, first_part, holed_portion), 'slab'), 'dp')  1360 us
    psum x1, waiting for transfers between devices, per_device(): lax.psum((point_part, first_part, holed_portion), 'slab')  116 us
  transfers between devices with their start and end apart: 8, of which 3 were waited for; matrix products, arithmetic and copies ran while one was open for 3% of the time, Pallas kernels for 0%

profile of v1, /device:TPU:8, one launch (start us, length us, event | category | flops | bytes accessed | tf_op | source)
XLA Modules:
  0.0 1618.4 jit_solution(5899261443336079528)
XLA Ops:
  7.2 0.8 fusion.39
  8.1 0.1 select_n.29
  8.2 1.2 fusion.33
  9.4 0.7 convolution_convert_fusion
  10.1 1.3 collective-permute-start.5
  11.4 12.9 collective-permute-start.4
  24.3 1.3 collective-permute-start
  25.6 1.3 collective-permute-start.1
  27.1 2.4 convert.10
  29.5 2.6 fusion.38
  32.1 13.2 fusion.40
  45.3 1.3 collective-permute-start.3
  46.6 10.8 collective-permute-start.2
  57.5 3.9 bitcast_convert_fusion
  61.3 29.4 %collective-permute-done.4 = bf16[1,12,40,2048]{3,2,1,0:T(8,128)(2,1)} collective-permute-done((bf16[1,12,40,2048]{3,2,1,0:T(8,128)(2,1)S(1)}, bf16[1,12,40,2048]{3,2,1,0:T(8,128)(2,1)}, u32[]{:S(2)}, u32[]{:S(2)}) %collective-permute-start.4) | collective-permute-done | bytes 1966112 | tf_op jit(solution)/shard_map/ppermute | solution.py:13
  90.7 3.9 bitcast_convert_fusion.1
  94.6 16.6 %fusion.23 = (f32[2048]{0:T(1024)S(1)}, f32[2048]{0:T(1024)S(1)}, f32[2048]{0:T(1024)S(1)}, f32[2048]{0:T(1024)S(1)}, f32[2048]{0:T(1024)S(1)}, /*index=5*/f32[2...) fusion(f32[14,40,2048]{2,1,0:T(8,128)} %get-tuple-element.39, ...), kind=kLoop, calls=%fused_computation.60 | loop fusion | flops 37337088 | bytes 30294016 | tf_op jit(solution)/shard_map/reduce_sum | solution.py:53
  111.2 0.1 stack.69
  111.4 0.7 reshape.75
  112.1 2.0 bitcast_convert_fusion.3
  114.1 2.2 bitcast_convert_fusion.2
  116.3 0.5 copy-done.1
  116.8 3.3 add_convert_fusion
  120.1 4.6 fusion.14
  124.7 0.1 stack.79
  124.8 0.7 reshape.76
  125.5 3.7 convolution_bitcast_fusion
  129.3 115.9 %all-reduce.14.cloned.1.call-done = (f32[2048,256]{1,0:T(8,128)}, f32[3,3,2048]{2,1,0:T(4,128)}, f32[3,3,2048]{2,1,0:T(4,128)}) async-done(((f32[2048,256]{1,0:T(8,128)}, f32[3,3,2048]{2,1,0:T(4,128)}, f32[3,3,2048]{2,1,0:T(4,128)}), (f32[2048,256]{1,0:T(8,128)}, f32[3,3,2048]{2,1,0:T(4,128)}, f32[3,3,2048]{2,1,0:T(4,128)})) %all-reduce.14.cloned.1.call-update) | async-done | bytes 2244624 | tf_op jit(solution)/shard_map/psum | solution.py:138
  245.2 1.4 convolution_convert_fusion.1
  246.5 1360.6 %all-reduce.12.cloned.1.call-done = (f32[2048,256]{1,0:T(8,128)}, f32[3,3,2048]{2,1,0:T(4,128)}, f32[3,3,2048]{2,1,0:T(4,128)}) async-done(((f32[2048,256]{1,0:T(8,128)}, f32[3,3,2048]{2,1,0:T(4,128)}, f32[3,3,2048]{2,1,0:T(4,128)}), (f32[2048,256]{1,0:T(8,128)}, f32[3,3,2048]{2,1,0:T(4,128)}, f32[3,3,2048]{2,1,0:T(4,128)})) %all-reduce.12.cloned.1.call-update) | async-done | bytes 2244624 | tf_op jit(solution)/shard_map/psum | solution.py:137
  1607.1 2.8 multiply_convert_fusion
  1609.9 1.7 broadcast_multiply_fusion
  (28 shorter events, 0.3 us)
Async XLA Ops:
  7.2 2.2 copy-start
  7.2 19.7 %copy-start.6 = (f32[3,3,2048]{2,1,0:T(4,128)S(1)}, f32[3,3,2048]{2,1,0:T(4,128)}, u32[]{:S(2)}) copy-start(f32[3,3,2048]{2,1,0:T(4,128)} %param.9) | copy-start | bytes 221188
  7.2 19.8 %copy-start.7 = (f32[3,3,2048]{2,1,0:T(4,128)S(1)}, f32[3,3,2048]{2,1,0:T(4,128)}, u32[]{:S(2)}) copy-start(f32[3,3,2048]{2,1,0:T(4,128)} %param.10) | copy-start | bytes 221188
  7.2 237.9 %all-reduce.14.cloned.1.call-start = ((), (), s32[]{:S(2)}) async-start(), calls=%async_computation.1 | async-start | bytes 4587520 | tf_op jit(solution)/shard_map/psum | solution.py:138
  8.1 16.2 copy-start.3
  10.1 47.3 %collective-permute-start.5 = (bf16[1,12,40,2048]{3,2,1,0:T(8,128)(2,1)S(1)}, bf16[1,12,40,2048]{3,2,1,0:T(8,128)(2,1)}, u32[]{:S(2)}, u32[]{:S(2)}) collective-permute-start(bf16[1,12,40,2048]{3,2,1,0:T(8,128)(2,1)S(1)} %bitcast.100), channel_id=1, source_target_pairs={{3,0},{7,4},{11,8},{15,12},{19,16},{23,20},{27,24},{31,28},{35,32}... | collective-permute-start | bytes 5898248 | tf_op jit(solution)/shard_map/ppermute | solution.py:13
  11.4 79.3 %collective-permute-start.4 = (bf16[1,12,40,2048]{3,2,1,0:T(8,128)(2,1)S(1)}, bf16[1,12,40,2048]{3,2,1,0:T(8,128)(2,1)}, u32[]{:S(2)}, u32[]{:S(2)}) collective-permute-start(bf16[1,12,40,2048]{3,2,1,0:T(8,128)(2,1)S(1)} %bitcast.101), channel_id=1, source_target_pairs={{0,3},{4,7},{8,11},{12,15},{16,19},{20,23},{24,27},{28,31},{32,35}... | collective-permute-start | bytes 5898248 | tf_op jit(solution)/shard_map/ppermute | solution.py:13
  24.3 5.1 collective-permute-start
  25.6 3.8 collective-permute-start.1
  45.3 68.8 %collective-permute-start.3 = (bf16[1,12,40,2048]{3,2,1,0:T(8,128)(2,1)}, bf16[1,12,40,2048]{3,2,1,0:T(8,128)(2,1)}, u32[]{:S(2)}, u32[]{:S(2)}) collective-permute-start(bf16[1,12,40,2048]{3,2,1,0:T(8,128)(2,1)} %bitcast.105), channel_id=1, source_target_pairs={{3,0},{7,4},{11,8},{15,12},{19,16},{23,20},{27,24},{31,28},{35,32}... | collective-permute-start | bytes 5898248 | tf_op jit(solution)/shard_map/ppermute | solution.py:13
  46.6 65.4 %collective-permute-start.2 = (bf16[1,12,40,2048]{3,2,1,0:T(8,128)(2,1)}, bf16[1,12,40,2048]{3,2,1,0:T(8,128)(2,1)}, u32[]{:S(2)}, u32[]{:S(2)}) collective-permute-start(bf16[1,12,40,2048]{3,2,1,0:T(8,128)(2,1)} %bitcast.106), channel_id=1, source_target_pairs={{0,3},{4,7},{8,11},{12,15},{16,19},{20,23},{24,27},{28,31},{32,35}... | collective-permute-start | bytes 5898248 | tf_op jit(solution)/shard_map/ppermute | solution.py:13
  114.1 2.7 copy-start.1
  116.8 3.3 copy-start.2
  120.1 5.4 copy-start.5
  129.2 116.0 %copy-start.4 = (bf16[12,40,2048]{2,1,0:T(8,128)(2,1)S(1)}, bf16[12,40,2048]{2,1,0:T(8,128)(2,1)}, u32[]{:S(2)}) copy-start(bf16[12,40,2048]{2,1,0:T(8,128)(2,1)} %add_convert_fusion) | copy-start | bytes 5898244
  129.2 1477.9 %all-reduce.12.cloned.1.call-start = ((), (), s32[]{:S(2)}) async-start(), calls=%async_computation | async-start | bytes 4587520 | tf_op jit(solution)/shard_map/psum | solution.py:137
Sparse Core Ops, SparseCore 0:
  129.4 115.7 all-reduce.13
  248.5 1358.5 all-reduce.11
